TPU v7x, 512 devices: a whole 4x4x16 slice. The times are simulated.
512 devices in a mesh: state: 8 (over x, core), vocab: 64 (over z, y).
Axes of the slice: x: 4, y: 4, z: 16, core: 2. Of those that a mesh axis runs over, the one named last changes fastest.
Arguments:
- token_ids: int32 [7680], P('vocab'), may hold values from 0 to 65535, as said below
- send_counts: int32 [4096], P('vocab'), may hold values from 0 to 5, as said below
- forward_rows: bfloat16 [7680, 16384], P('vocab', 'state'), may hold values from 0.01 to 32, as said below
- backward_rows: bfloat16 [7680, 16384], P('vocab', 'state'), may hold values from 0.01 to 32, as said below
Outputs:
- emission_counts: bfloat16 [16384, 65536], P('state', 'vocab')
Inputs may be any that keep to these rules, and one draw needn't show every extreme that they name: `token_ids`: within each aligned block of 120 positions the ids never fall; at most 5 ids of a block lie in one range of 1024 ids (k * 1024 to (k + 1) * 1024 - 1), and at most 3 distinct ids; in every block some range holds exactly 5 ids with exactly 3 distinct ones, and one range holds exactly 5 in every block. `send_counts`: entry b * 64 + k is the number of ids of block b in range k; each block's entries sum to 120. `forward_rows`: positive. `backward_rows`: positive.
All inputs are finite; a program needn't handle non-finite values.
Results may differ from a plain program's by a relative error of at most 0.0095.
Values may be sent and summed in bfloat16 or wider, within the bound.
A program may use at most 64 MiB of HBM per device.

v0:
```python
import jax
import jax.numpy as jnp
from jax import lax
from jax.sharding import PartitionSpec as P

V_DEV = 1024


def merge_lanes(rows, cols, lanes_out):
    valid = cols >= 0
    before = jnp.concatenate([jnp.full((cols.shape[0], 1), -2, jnp.int32), cols[:, :-1]], axis=1)
    change = jnp.logical_and(valid, cols != before)
    group = jnp.cumsum(change.astype(jnp.int32), axis=1) - 1
    slots = jnp.arange(lanes_out, dtype=jnp.int32)
    pick = jnp.logical_and(group[:, :, None] == slots[None, None, :], valid[:, :, None])
    merged = jnp.einsum(
        "ncl,ncs->nls", pick.astype(jnp.bfloat16), rows, preferred_element_type=jnp.float32
    )
    leading = jnp.logical_and(pick, change[:, :, None])
    found = jnp.any(leading, axis=1)
    picked_cols = jnp.sum(leading.astype(jnp.int32) * cols[:, :, None], axis=1)
    merged_cols = jnp.where(found, picked_cols, -1)
    return (merged.astype(jnp.bfloat16), merged_cols)


def shards(token_ids, send_counts, forward_rows, backward_rows):
    owners = lax.axis_size("vocab")
    width = forward_rows.shape[1]
    count_rows = token_ids.shape[0]
    limit = max(2, (8 * count_rows + 3 * owners - 1) // (3 * owners))
    nstates = width * lax.axis_size("state")
    weights = (forward_rows.astype(jnp.float32) * backward_rows.astype(jnp.float32)).astype(
        jnp.bfloat16
    )
    partial_value = jnp.sum(weights.astype(jnp.float32), axis=1)
    ends = jnp.cumsum(send_counts)
    starts = ends - send_counts
    lanes = jnp.arange(limit, dtype=jnp.int32)
    valid = lanes[None, :] < send_counts[:, None]
    source = jnp.clip(starts[:, None] + lanes[None, :], 0, count_rows - 1)
    columns = jnp.where(valid, token_ids[source] % V_DEV, -1)
    blank = jnp.zeros((), jnp.bfloat16)
    total = lax.psum(partial_value, "state")
    posterior = (weights.astype(jnp.float32) * (nstates / total)[:, None]).astype(jnp.bfloat16)
    outgoing = jnp.where(valid[:, :, None], posterior[source], blank)
    merged, merged_cols = merge_lanes(outgoing, columns, limit)
    gamma, arrived_cols = (
        lax.all_to_all(merged, "vocab", split_axis=0, concat_axis=0, tiled=True),
        lax.all_to_all(merged_cols, "vocab", split_axis=0, concat_axis=0, tiled=True),
    )
    onehot = (arrived_cols[:, :, None] == jnp.arange(V_DEV, dtype=jnp.int32)[None, None, :]).astype(
        jnp.bfloat16
    )
    counts = lax.dot_general(
        gamma, onehot, (((0, 1), (0, 1)), ((), ())), preferred_element_type=jnp.float32
    )
    return counts.astype(jnp.bfloat16)


def solution(mesh):
    placed = (P("vocab"), P("vocab"), P("vocab", "state"), P("vocab", "state"))
    return jax.shard_map(
        shards, mesh=mesh, in_specs=placed, out_specs=P("state", "vocab"), check_vma=False
    )
```

profile of v0, /device:TPU:24, one launch (start us, length us, event | category | flops | bytes accessed | tf_op | source)
XLA Modules:
  0.0 164.3 jit_solution(6843603864691174391)
XLA Ops:
  0.0 0.0 copy-start
  0.0 0.8 copy.13
  0.8 0.1 reduce-window.9
  0.9 0.1 reduce
  1.0 0.7 sub.7
  1.6 0.1 compare_select_fusion
  1.7 0.1 reshape.170
  1.9 0.0 copy-done
  1.9 0.0 copy-start.3
  1.9 0.0 copy-start.1
  1.9 0.0 copy-start.2
  1.9 2.4 %gather_fusion = s32[320]{0:T(512)S(1)} fusion(s32[120]{0:T(128)S(1)} %copy-done, s32[1024]{0:T(1024)S(1)} %pad_clamp_fusion), kind=kCustom, calls=%fused_computation | custom fusion | bytes 3840 | tf_op jit(solution)/shard_map/gather | solution.py:41
  4.3 0.1 reshape.169
  4.4 0.0 copy-done.3
  4.4 0.1 broadcast_compare_fusion
  4.5 0.1 fusion.17
  4.6 0.2 reduce_window_sum.18
  4.8 1.2 select_reduce_fusion
  5.9 1.2 fusion.9
  7.1 0.6 broadcast_select_fusion
  7.7 18.5 %all-to-all-start.1 = ((s32[64,1,5]{2,1,0:T(1,128)}), s32[64,1,5]{2,1,0:T(1,128)S(1)}, u32[]{:S(2)}, u32[]{:S(2)}) async-start(s32[64,1,5]{2,1,0:T(1,128)} %bitcast.2), calls=%async_computation.1 | async-start | bytes 65536 | tf_op jit(solution)/shard_map/all_to_all | solution.py:49
  26.2 0.0 copy-done.1
  26.3 0.0 copy-done.2
  26.3 0.2 convert_reduce_fusion
  26.5 14.6 %psum.7 = f32[120]{0:T(128)S(1)} all-reduce(f32[120]{0:T(128)S(1)} %convert_reduce_fusion), channel_id=1, replica_groups=mesh['state'=8,'vocab'=64] {'state'}, use_global_device_ids=true, to_apply=%region_3.4 | all-reduce | flops 120 | bytes 960 | tf_op jit(solution)/shard_map/psum | solution.py:43
  41.1 0.2 fusion.4
  41.3 2.4 %gather_fusion.1 = bf16[320,2048]{1,0:T(8,128)(2,1)S(1)} fusion(bf16[120,2048]{1,0:T(8,128)(2,1)S(1)} %fusion.4, s32[1024]{0:T(1024)S(1)} %pad_clamp_fusion), kind=kCustom, calls=%fused_computation.1 | custom fusion | bytes 2622720 | tf_op jit(solution)/shard_map/gather | solution.py:45
  43.7 0.6 reshape.177
  44.3 2.1 %convolution_convert_fusion = bf16[64,5,2048]{2,1,0:T(8,128)(2,1)} fusion(bf16[64,5,2048]{2,1,0:T(8,128)(2,1)S(1)} %reshape.177, pred[64,5]{1,0:T(8,128)(4,1)S(1)} %get-tuple-element.9, s32[64,5]{1,0:T(8,128)S(1)} %broadcast_add_fusion, pred[64,5]{1,0:T(8,128)(4,1)S(1)} %get-tuple-element.5), kind=kOutput, calls=%fused_computation.3 | convolution fusion | flops 7867520 | bytes 2623360 | tf_op jit(solution)/shard_map/ncl,ncs->nls/dot_general | solution.py:16
  46.4 0.0 all-to-all-done.1
  46.4 14.5 %all-to-all-start = ((bf16[64,5,2048]{2,1,0:T(8,128)(2,1)}), bf16[64,5,2048]{2,1,0:T(8,128)(2,1)S(1)}, u32[]{:S(2)}, u32[]{:S(2)}) async-start(bf16[64,5,2048]{2,1,0:T(8,128)(2,1)} %convolution_convert_fusion), calls=%async_computation | async-start | bytes 4194304 | tf_op jit(solution)/shard_map/all_to_all | solution.py:48
  60.9 0.1 copy.15
  61.0 98.5 %all-to-all-done = bf16[64,5,2048]{2,1,0:T(8,128)(2,1)S(1)} async-done(((bf16[64,5,2048]{2,1,0:T(8,128)(2,1)}), bf16[64,5,2048]{2,1,0:T(8,128)(2,1)S(1)}, u32[]{:S(2)}, u32[]{:S(2)}) %all-to-all-start) | async-done | bytes 1310752 | tf_op jit(solution)/shard_map/all_to_all | solution.py:48
  159.5 4.9 %bitcast_convert_fusion = bf16[2048,1024]{1,0:T(8,128)(2,1)} fusion(bf16[64,5,2048]{2,1,0:T(8,128)(2,1)S(1)} %all-to-all-done, s32[64,5]{0,1:T(8,128)S(1)} %copy.15), kind=kOutput, calls=%fused_computation.2 | convolution fusion | flops 1344602112 | bytes 5506304 | tf_op jit(solution)/shard_map/dot_general | solution.py:54
  (3 shorter events, 0.0 us)
Async XLA Ops:
  0.0 1.9 %copy-start = (s32[120]{0:T(128)S(1)}, s32[120]{0:T(128)}, u32[]{:S(2)}) copy-start(s32[120]{0:T(128)} %param.4) | copy-start | bytes 1444
  1.9 2.5 %copy-start.3 = (s32[64]{0:T(128)S(1)}, s32[64]{0:T(128)}, u32[]{:S(2)}) copy-start(s32[64]{0:T(128)} %param.5) | copy-start | bytes 772
  1.9 24.4 %copy-start.1 = (bf16[120,2048]{1,0:T(8,128)(2,1)S(1)}, bf16[120,2048]{1,0:T(8,128)(2,1)}, u32[]{:S(2)}) copy-start(bf16[120,2048]{1,0:T(8,128)(2,1)} %param.7) | copy-start | bytes 1474564
  1.9 24.4 %copy-start.2 = (bf16[120,2048]{1,0:T(8,128)(2,1)S(1)}, bf16[120,2048]{1,0:T(8,128)(2,1)}, u32[]{:S(2)}) copy-start(bf16[120,2048]{1,0:T(8,128)(2,1)} %param.6) | copy-start | bytes 1474564
  7.7 38.7 %all-to-all-start.1 = ((s32[64,1,5]{2,1,0:T(1,128)}), s32[64,1,5]{2,1,0:T(1,128)S(1)}, u32[]{:S(2)}, u32[]{:S(2)}) async-start(s32[64,1,5]{2,1,0:T(1,128)} %bitcast.2), calls=%async_computation.1 | async-start | bytes 65536 | tf_op jit(solution)/shard_map/all_to_all | solution.py:49
  46.4 113.1 %all-to-all-start = ((bf16[64,5,2048]{2,1,0:T(8,128)(2,1)}), bf16[64,5,2048]{2,1,0:T(8,128)(2,1)S(1)}, u32[]{:S(2)}, u32[]{:S(2)}) async-start(bf16[64,5,2048]{2,1,0:T(8,128)(2,1)} %convolution_convert_fusion), calls=%async_computation | async-start | bytes 4194304 | tf_op jit(solution)/shard_map/all_to_all | solution.py:48
where the time goes:
time: 165 us; the launch traced here: 164 us
  waiting for transfers between devices  98.5 us (60%)
  starting transfers between devices  33 us (20%)
  blocking collectives  14.6 us (9%)
  matrix products  6.97 us (4%)
  local copies, waits for them, and re-layouts  6.46 us (4%)
  other arithmetic  4.63 us (3%)
    all_to_all x1, waiting for transfers between devices, shards(): lax.all_to_all(merged, 'vocab', split_axis=0, concat_axis=0, tiled=True)  98.5 us
    all_to_all x1, starting transfers between devices, shards(): lax.all_to_all(merged_cols, 'vocab', split_axis=0, concat_axis=0, tiled=T...  18.5 us
    psum x1, blocking collectives, shards(): total = lax.psum(partial_value, 'state')  14.6 us
    all_to_all x1, starting transfers between devices, shards(): lax.all_to_all(merged, 'vocab', split_axis=0, concat_axis=0, tiled=True)  14.5 us
    dot_general x1, matrix products, shards(): lax.dot_general(gamma, onehot, (((0, 1), (0, 1)), ((), ())), preferred_el...  4.87 us
  transfers between devices with their start and end apart: 2, of which 1 were waited for; matrix products, arithmetic and copies ran while one was open for 3% of the time, Pallas kernels for 0%

commit v1 on v0

v1 whole, which is shorter than its diff:
```python
import functools

import jax
import jax.numpy as jnp
from jax import lax
from jax.experimental import pallas as pl
from jax.experimental.pallas import tpu as pltpu
from jax.sharding import PartitionSpec as P

V_DEV = 1024
LANES = 128
SIDE = 4
MESH = pl.DeviceIdType.MESH
F32 = jnp.float32
BF16 = jnp.bfloat16


def peer(i, z, y, depth):
    q = i // SIDE
    h = (q + 1) // 2
    dz = lax.rem(depth // 2 + h * (1 - 2 * lax.rem(q, 2)) + depth, depth)
    dy = lax.rem(i, SIDE) + q // (depth - 1)
    there = lax.rem(z + dz, depth) * SIDE + lax.rem(y + dy, SIDE)
    return there, dz * SIDE + dy


def route(token_row):
    n = token_row.shape[1]
    ids = token_row.astype(F32)
    up = lax.broadcasted_iota(jnp.int32, (n, n), 0)
    across = lax.broadcasted_iota(jnp.int32, (n, n), 1)
    eye = up == across
    before = up < across

    def turn(row):
        return jnp.sum(jnp.where(eye, row, 0.0), axis=1, keepdims=True)

    ids_col = turn(ids)
    owner = jnp.floor(ids * (1.0 / V_DEV))
    owner_col = jnp.floor(ids_col * (1.0 / V_DEV))
    same_id = jnp.where(ids_col == ids, 1.0, 0.0)
    same_owner = jnp.where(owner_col == owner, 1.0, 0.0)
    earlier = jnp.where(before, 1.0, 0.0)
    alone = jnp.where(jnp.sum(same_id, axis=0, keepdims=True) == 1.0, 1.0, 0.0)
    alone_before = jnp.sum(same_owner * earlier * turn(alone), axis=0, keepdims=True)
    raw = jnp.where(alone_before == 0.0, alone, 0.0)
    repeats = jnp.sum(same_id * earlier, axis=0, keepdims=True)
    leads = jnp.where(repeats == 0.0, 1.0 - raw, 0.0)
    lower = jnp.where(ids_col < ids, 1.0, 0.0)
    rank = jnp.sum(same_owner * lower * turn(leads), axis=0, keepdims=True)
    slot = jnp.where(raw == 1.0, 0.0, 1.0 + rank)
    first = jnp.where(repeats == 0.0, 1.0, 0.0)
    return owner, ids - owner * V_DEV, slot, first


def lay(rows, wide, out, base):
    k, width = rows.shape
    parts = width // LANES
    for i in range(parts):
        wide[pl.ds(i, k, stride=parts), :] = rows[:, i * LANES : (i + 1) * LANES]
    out[:, base : base + parts, :] = wide[...].reshape(k, parts, LANES).astype(BF16)


def exchange(
    owners,
    ranks,
    token_ref,
    forward_ref,
    backward_ref,
    got_raw,
    got_pair,
    got_meta,
    weights,
    wide,
    send_raw,
    send_pair,
    send_meta,
    sums,
    norm_send,
    norm_recv,
    raw_send,
    raw_recv,
    pair_send,
    pair_recv,
    meta_send,
    meta_recv,
    own_sem,
):
    depth = owners // SIDE
    me = lax.axis_index("vocab")
    rank = lax.axis_index("state")
    z, y = me // SIDE, lax.rem(me, SIDE)
    parts = send_raw.shape[1]

    barrier = pltpu.get_barrier_semaphore()

    def greet(i, carry):
        there, _ = peer(i, z, y, depth)
        pl.semaphore_signal(barrier, inc=1, device_id={"vocab": there}, device_id_type=MESH)
        return carry

    lax.fori_loop(0, owners - 1, greet, 0)
    for d in range(1, ranks):
        other = lax.rem(rank + d, ranks)
        pl.semaphore_signal(barrier, inc=1, device_id={"state": other}, device_id_type=MESH)

    weights[...] = (forward_ref[...].astype(F32) * backward_ref[...].astype(F32)).astype(BF16)
    count, width = weights.shape
    partial = lax.dot_general(
        jnp.ones((8, width), BF16), weights[...], (((1,), (1,)), ((), ())), preferred_element_type=F32
    )
    sums[rank] = partial[:1]
    owner, column, slot, first = route(token_ref[...])
    owner_of = lax.broadcasted_iota(jnp.int32, (owners, count), 0).astype(F32)
    mine = owner_of == owner
    picks = [jnp.where(jnp.logical_and(mine, slot == s), 1.0, 0.0) for s in (0.0, 1.0, 2.0)]
    raw = jnp.dot(picks[0].astype(BF16), weights[...], preferred_element_type=F32)
    lay(raw, wide, send_raw, 0)

    pl.semaphore_wait(barrier, owners - 1 + ranks - 1)

    for d in range(1, ranks):
        other = lax.rem(rank + d, ranks)
        pltpu.make_async_remote_copy(
            src_ref=sums.at[rank],
            dst_ref=sums.at[rank],
            send_sem=norm_send,
            recv_sem=norm_recv.at[d - 1],
            device_id={"state": other},
            device_id_type=MESH,
        ).start()

    def push_raw(i, carry):
        there, offset = peer(i, z, y, depth)
        pltpu.make_async_remote_copy(
            src_ref=send_raw.at[there],
            dst_ref=got_raw.at[offset],
            send_sem=raw_send,
            recv_sem=raw_recv,
            device_id={"vocab": there},
            device_id_type=MESH,
        ).start()
        return carry

    lax.fori_loop(0, owners - 1, push_raw, 0)
    own_raw = pltpu.make_async_copy(send_raw.at[me], got_raw.at[0], own_sem.at[0])
    own_raw.start()

    for d in range(1, ranks):
        source = lax.rem(rank + ranks - d, ranks)
        pltpu.make_async_copy(sums.at[source], sums.at[source], norm_recv.at[d - 1]).wait()
    total = sums[0]
    for d in range(1, ranks):
        total = total + sums[d]
    scale = (ranks * width) / total
    eye = lax.broadcasted_iota(jnp.int32, (count, count), 0) == lax.broadcasted_iota(
        jnp.int32, (count, count), 1
    )
    scale_col = jnp.sum(jnp.where(eye, scale, 0.0), axis=1, keepdims=True)
    posterior = (weights[...].astype(F32) * scale_col).astype(BF16)
    for s in (1, 2):
        merged = jnp.dot(picks[s].astype(BF16), posterior, preferred_element_type=F32)
        lay(merged, wide, send_pair, (s - 1) * parts)
    lane = lax.broadcasted_iota(jnp.int32, (owners, LANES), 1)
    meta = jnp.zeros((owners, LANES), F32)
    for s in range(3):
        here = picks[s] * first
        ids = jnp.sum(here * (column + 1.0), axis=1, keepdims=True) - 1.0
        meta = jnp.where(lane == s, ids, meta)
    meta = jnp.where(lane == 3, jnp.sum(picks[0] * scale, axis=1, keepdims=True), meta)
    send_meta[...] = meta.reshape(owners, 1, LANES)

    def push_pair(i, carry):
        there, offset = peer(i, z, y, depth)
        pltpu.make_async_remote_copy(
            src_ref=send_pair.at[there],
            dst_ref=got_pair.at[offset],
            send_sem=pair_send,
            recv_sem=pair_recv,
            device_id={"vocab": there},
            device_id_type=MESH,
        ).start()
        pltpu.make_async_remote_copy(
            src_ref=send_meta.at[there],
            dst_ref=got_meta.at[offset],
            send_sem=meta_send,
            recv_sem=meta_recv,
            device_id={"vocab": there},
            device_id_type=MESH,
        ).start()
        return carry

    lax.fori_loop(0, owners - 1, push_pair, 0)
    own_pair = pltpu.make_async_copy(send_pair.at[me], got_pair.at[0], own_sem.at[1])
    own_pair.start()
    own_meta = pltpu.make_async_copy(send_meta.at[me], got_meta.at[0], own_sem.at[2])
    own_meta.start()

    own_raw.wait()
    own_pair.wait()
    own_meta.wait()
    rest = pl.ds(1, owners - 1)
    for ref, sem in ((got_raw, raw_recv), (got_pair, pair_recv), (got_meta, meta_recv)):
        pltpu.make_async_copy(ref.at[rest], ref.at[rest], sem).wait()
    for ref, sem in ((send_raw, raw_send), (send_pair, pair_send), (send_meta, meta_send)):
        pltpu.make_async_copy(ref.at[rest], ref.at[rest], sem).wait()
    others = pl.ds(1, ranks - 1)
    pltpu.make_async_copy(sums.at[others], sums.at[others], norm_send).wait()


def place(raw_ref, pair_ref, meta_ref, out_ref, wide_raw, wide_pair, onehot, block, sems):
    owners, parts, _ = raw_ref.shape
    wide_raw[...] = raw_ref[...].reshape(owners * parts, LANES).astype(F32)
    wide_pair[...] = pair_ref[...].reshape(owners * 2 * parts, LANES).astype(F32)
    meta = meta_ref[...].reshape(owners, LANES)
    ids = lax.broadcasted_iota(jnp.int32, (owners, V_DEV), 1).astype(F32)
    for s in range(3):
        hit = jnp.where(meta[:, s : s + 1] == ids, 1.0, 0.0)
        onehot[s * owners : (s + 1) * owners, :] = hit.astype(BF16)
    scale = meta[:, 3:4]
    copies = []
    for i in range(parts):
        lone = wide_raw[pl.ds(i, owners, stride=parts), :] * scale
        one = wide_pair[pl.ds(i, owners, stride=2 * parts), :]
        two = wide_pair[pl.ds(parts + i, owners, stride=2 * parts), :]
        rows = jnp.concatenate([lone.astype(BF16), one.astype(BF16), two.astype(BF16)], axis=0)
        counts = lax.dot_general(
            rows, onehot[...], (((0,), (0,)), ((), ())), preferred_element_type=F32
        )
        here = pl.ds(i * LANES, LANES)
        block[here, :] = counts.astype(BF16)
        copy = pltpu.make_async_copy(block.at[here], out_ref.at[here], sems.at[i])
        copy.start()
        copies.append(copy)
    for copy in copies:
        copy.wait()


def shards(token_ids, send_counts, forward_rows, backward_rows):
    owners = lax.axis_size("vocab")
    ranks = lax.axis_size("state")
    count, width = forward_rows.shape
    parts = width // LANES
    vmem = pl.BlockSpec(memory_space=pltpu.VMEM)
    anywhere = pl.BlockSpec(memory_space=pl.ANY)
    dma = pltpu.SemaphoreType.DMA
    got = pl.pallas_call(
        functools.partial(exchange, owners, ranks),
        out_shape=(
            jax.ShapeDtypeStruct((owners, parts, LANES), BF16),
            jax.ShapeDtypeStruct((owners, 2 * parts, LANES), BF16),
            jax.ShapeDtypeStruct((owners, 1, LANES), F32),
        ),
        in_specs=[vmem] * 3,
        out_specs=(anywhere,) * 3,
        scratch_shapes=[
            pltpu.VMEM((count, width), BF16),
            pltpu.VMEM((owners * parts, LANES), F32),
            pltpu.VMEM((owners, parts, LANES), BF16),
            pltpu.VMEM((owners, 2 * parts, LANES), BF16),
            pltpu.VMEM((owners, 1, LANES), F32),
            pltpu.VMEM((ranks, 1, count), F32),
            dma,
            dma((ranks - 1,)),
            dma,
            dma,
            dma,
            dma,
            dma,
            dma,
            dma((3,)),
        ],
        compiler_params=pltpu.CompilerParams(
            collective_id=0, has_side_effects=True, vmem_limit_bytes=32 * 1024 * 1024
        ),
    )(token_ids.reshape(1, count), forward_rows, backward_rows)
    return pl.pallas_call(
        place,
        out_shape=jax.ShapeDtypeStruct((width, V_DEV), BF16),
        in_specs=[vmem] * 3,
        out_specs=anywhere,
        scratch_shapes=[
            pltpu.VMEM((owners * parts, LANES), F32),
            pltpu.VMEM((owners * 2 * parts, LANES), F32),
            pltpu.VMEM((3 * owners, V_DEV), BF16),
            pltpu.VMEM((width, V_DEV), BF16),
            dma((parts,)),
        ],
        compiler_params=pltpu.CompilerParams(vmem_limit_bytes=32 * 1024 * 1024),
    )(*got)


def solution(mesh):
    placed = (P("vocab"), P("vocab"), P("vocab", "state"), P("vocab", "state"))
    return jax.shard_map(
        shards, mesh=mesh, in_specs=placed, out_specs=P("state", "vocab"), check_vma=False
    )
```

time: 165 us -> 61.1 us (0.37)
  waiting for transfers between devices: 98.5 us -> 0 us
  Pallas kernels: 0 us -> 57.2 us
  starting transfers between devices: 33 us -> 0 us
  blocking collectives: 14.6 us -> 0 us
  matrix products: 6.97 us -> 0 us
  other arithmetic: 4.63 us -> 0 us
  local copies, waits for them, and re-layouts: 6.46 us -> 2.71 us
    all_to_all x2 -> x0, waiting for transfers between devices: 98.5 us -> none  [the longest x1 98.5 us: shards(): lax.all_to_all(merged, 'vocab', split_axis=0, concat_axis=0, tiled=True)]
    pallas_call x0 -> x2, Pallas kernels: none -> 57.2 us  [the longest x1 53.8 us: shards(): pl.pallas_call(functools.partial(exchange, owners, ranks), out_shape=(jax...]
    all_to_all x2 -> x0, starting transfers between devices: 33 us -> none  [the longest x1 18.5 us: shards(): lax.all_to_all(merged_cols, 'vocab', split_axis=0, concat_axis=0, tiled=T...]
    psum x1 -> x0, blocking collectives: 14.6 us -> none  [shards(): total = lax.psum(partial_value, 'state')]
    dot_general x2 -> x0, matrix products: 6.97 us -> none  [the longest x1 4.87 us: shards(): lax.dot_general(gamma, onehot, (((0, 1), (0, 1)), ((), ())), preferred_el...]
    gather x4 -> x0, local copies, waits for them, and re-layouts: 5.48 us -> none  [the longest x2 2.99 us: shards(): outgoing = jnp.where(valid[:, :, None], posterior[source], blank)]
    unnamed x8 -> x6, local copies, waits for them, and re-layouts: 0.02 us -> 2.71 us
  transfers between devices with their start and end apart: 2 -> 0, of which waited for: 1 -> 0; matrix products, arithmetic and copies ran while one was open for 3% -> 0% of each run, Pallas kernels for 0% -> 0%
where the time goes in v1:
time: 61.1 us; the launch traced here: 60 us
  Pallas kernels  57.2 us (94%)
  local copies, waits for them, and re-layouts  2.71 us (4%)
    pallas_call x1, Pallas kernels, shards(): pl.pallas_call(functools.partial(exchange, owners, ranks), out_shape=(jax...  53.8 us
    pallas_call x1, Pallas kernels, shards(): pl.pallas_call(place, out_shape=jax.ShapeDtypeStruct((width, V_DEV), BF16...  3.44 us
    unnamed x6, local copies, waits for them, and re-layouts  2.71 us

profile of v1, /device:TPU:24, one launch (start us, length us, event | category | flops | bytes accessed | tf_op | source)
XLA Modules:
  0.0 60.0 jit_solution(12264570723086518120)
XLA Ops:
  0.0 0.0 copy-start
  0.0 1.0 %copy-done = bf16[120,2048]{1,0:T(8,128)(2,1)S(1)} copy-done((bf16[120,2048]{1,0:T(8,128)(2,1)S(1)}, bf16[120,2048]{1,0:T(8,128)(2,1)}, u32[]{:S(2)}) %copy-start) | copy-done | bytes 491544
  1.0 0.0 copy-start.1
  1.0 1.0 %copy-done.1 = bf16[120,2048]{1,0:T(8,128)(2,1)S(1)} copy-done((bf16[120,2048]{1,0:T(8,128)(2,1)S(1)}, bf16[120,2048]{1,0:T(8,128)(2,1)}, u32[]{:S(2)}) %copy-start.1) | copy-done | bytes 491544
  2.1 0.0 copy-start.2
  2.1 0.7 %copy-done.2 = s32[120]{0:T(128)S(1)} copy-done((s32[120]{0:T(128)S(1)}, s32[120]{0:T(128)}, u32[]{:S(2)}) %copy-start.2) | copy-done | bytes 504
  2.7 53.8 %shard_map.37 = (bf16[64,16,128]{2,1,0:T(8,128)(2,1)S(1)}, bf16[64,32,128]{2,1,0:T(8,128)(2,1)S(1)}, f32[64,1,128]{2,1,0:T(1,128)S(1)}) custom-call(s32[1,120]{1,0:T(1,128)S(1)} %bitcast.1, bf16[120,2048]{1,0:T(8,128)(2,1)S(1)} %copy-done, bf16[120,2048]{1,0:T(8,128)(2,1)S(1)} %copy-done.1), custom_call_target="tpu_custom_call" | custom-call | tf_op jit(solution)/shard_map/pallas_call | solution.py:247
  56.5 3.4 %shard_map.38 = bf16[2048,1024]{1,0:T(8,128)(2,1)} custom-call(bf16[64,16,128]{2,1,0:T(8,128)(2,1)S(1)} %get-tuple-element.8.raw_ref, bf16[64,32,128]{2,1,0:T(8,128)(2,1)S(1)} %get-tuple-element.9.pair_ref, f32[64,1,128]{2,1,0:T(1,128)S(1)} %get-tuple-element.10.meta_ref), custom_call_target="tpu_custom_call" | custom-call | tf_op jit(solution)/shard_map/pallas_call | solution.py:277
Async XLA Ops:
  0.0 1.0 %copy-start = (bf16[120,2048]{1,0:T(8,128)(2,1)S(1)}, bf16[120,2048]{1,0:T(8,128)(2,1)}, u32[]{:S(2)}) copy-start(bf16[120,2048]{1,0:T(8,128)(2,1)} %forward_ref.1) | copy-start | bytes 1474564
  1.0 1.0 %copy-start.1 = (bf16[120,2048]{1,0:T(8,128)(2,1)S(1)}, bf16[120,2048]{1,0:T(8,128)(2,1)}, u32[]{:S(2)}) copy-start(bf16[120,2048]{1,0:T(8,128)(2,1)} %backward_ref.1) | copy-start | bytes 1474564
  2.1 0.7 %copy-start.2 = (s32[120]{0:T(128)S(1)}, s32[120]{0:T(128)}, u32[]{:S(2)}) copy-start(s32[120]{0:T(128)} %param.4) | copy-start | bytes 1444

commit v2 on v1

--- a/solution.py
+++ b/solution.py
@@ -15,13 +15,14 @@
 BF16 = jnp.bfloat16
 
 
-def peer(i, z, y, depth):
-    q = i // SIDE
-    h = (q + 1) // 2
-    dz = lax.rem(depth // 2 + h * (1 - 2 * lax.rem(q, 2)) + depth, depth)
-    dy = lax.rem(i, SIDE) + q // (depth - 1)
-    there = lax.rem(z + dz, depth) * SIDE + lax.rem(y + dy, SIDE)
-    return there, dz * SIDE + dy
+def target(k, z, half, to_late):
+    late = z // half
+    h = (k + 1) // 2
+    turn = h * (1 - 2 * lax.rem(k, 2)) + 2 * half
+    if to_late:
+        return half + lax.rem(z + turn + late * (half // 2), half)
+    ranked = lax.rem(k, 2) * (half // 2) + k // 2
+    return (1 - late) * lax.rem(z + turn + half // 2, half) + late * ranked
 
 
 def route(token_row):
@@ -70,6 +71,9 @@
     got_raw,
     got_pair,
     got_meta,
+    token,
+    forward,
+    backward,
     weights,
     wide,
     send_raw,
@@ -85,6 +89,9 @@
     meta_send,
     meta_recv,
     own_sem,
+    load_sem,
+    column_in,
+    late_in,
 ):
     depth = owners // SIDE
     me = lax.axis_index("vocab")
@@ -92,33 +99,105 @@
     z, y = me // SIDE, lax.rem(me, SIDE)
     parts = send_raw.shape[1]
 
+    loads = [
+        pltpu.make_async_copy(source, here, load_sem.at[i])
+        for i, (source, here) in enumerate(
+            ((token_ref, token), (forward_ref, forward), (backward_ref, backward))
+        )
+    ]
+    for load in loads:
+        load.start()
+
+    half = depth // 2
+    late = z // half
+    ys = [lax.rem(y + dy, SIDE) for dy in range(SIDE)]
+
     barrier = pltpu.get_barrier_semaphore()
 
-    def greet(i, carry):
-        there, _ = peer(i, z, y, depth)
-        pl.semaphore_signal(barrier, inc=1, device_id={"vocab": there}, device_id_type=MESH)
-        return carry
-
-    lax.fori_loop(0, owners - 1, greet, 0)
+    def greet(**where):
+        pl.semaphore_signal(barrier, inc=1, device_id=where, device_id_type=MESH)
+
+    for dz in range(1, half):
+        greet(vocab=(late * half + lax.rem(z + dz, half)) * SIDE + y)
+
+    @pl.when(late == 0)
+    def _():
+        for k in range(half):
+            greet(vocab=(half + k) * SIDE + y)
+
+    for dy in range(1, SIDE):
+        greet(vocab=z * SIDE + ys[dy])
     for d in range(1, ranks):
-        other = lax.rem(rank + d, ranks)
-        pl.semaphore_signal(barrier, inc=1, device_id={"state": other}, device_id_type=MESH)
-
-    weights[...] = (forward_ref[...].astype(F32) * backward_ref[...].astype(F32)).astype(BF16)
+        greet(state=lax.rem(rank + d, ranks))
+
+    loads[0].wait()
     count, width = weights.shape
-    partial = lax.dot_general(
-        jnp.ones((8, width), BF16), weights[...], (((1,), (1,)), ((), ())), preferred_element_type=F32
-    )
-    sums[rank] = partial[:1]
-    owner, column, slot, first = route(token_ref[...])
+    owner, column, slot, first = route(token[...])
     owner_of = lax.broadcasted_iota(jnp.int32, (owners, count), 0).astype(F32)
     mine = owner_of == owner
     picks = [jnp.where(jnp.logical_and(mine, slot == s), 1.0, 0.0) for s in (0.0, 1.0, 2.0)]
+    loads[1].wait()
+    loads[2].wait()
+    weights[...] = (forward[...].astype(F32) * backward[...].astype(F32)).astype(BF16)
     raw = jnp.dot(picks[0].astype(BF16), weights[...], preferred_element_type=F32)
     lay(raw, wide, send_raw, 0)
 
-    pl.semaphore_wait(barrier, owners - 1 + ranks - 1)
-
+    partial = lax.dot_general(
+        jnp.ones((8, width), BF16), weights[...], (((1,), (1,)), ((), ())), preferred_element_type=F32
+    )
+    sums[rank] = partial[:1]
+
+    def push(sources, k, dys, to_late):
+        there_z = target(k, z, half, to_late)
+        dz = lax.rem(there_z - z + depth, depth)
+        for dy in dys:
+            there = there_z * SIDE + ys[dy]
+            for source, landing, sent, landed in sources:
+                pltpu.make_async_remote_copy(
+                    src_ref=source.at[there],
+                    dst_ref=landing.at[dz * SIDE + dy],
+                    send_sem=sent,
+                    recv_sem=landed,
+                    device_id={"vocab": there},
+                    device_id_type=MESH,
+                ).start()
+
+    def push_half(sources, dys, to_late, unroll):
+        def step(k, carry):
+            push(sources, k, dys, to_late)
+            return carry
+
+        if unroll:
+            for k in range(half - 1):
+                push(sources, k, dys, to_late)
+        else:
+            lax.fori_loop(0, half - 1, step, 0)
+        push(sources, half - 1, [dy for dy in dys if dy], to_late)
+        if 0 in dys:
+
+            @pl.when(late != int(to_late))
+            def _():
+                push(sources, half - 1, [0], to_late)
+
+    raw_ways = ((send_raw, got_raw, raw_send, raw_recv),)
+    pair_ways = (
+        (send_pair, got_pair, pair_send, pair_recv),
+        (send_meta, got_meta, meta_send, meta_recv),
+    )
+
+    @pl.when(late == 0)
+    def _():
+        pl.semaphore_wait(barrier, half - 1 + SIDE - 1 + ranks - 1)
+
+    @pl.when(late != 0)
+    def _():
+        pl.semaphore_wait(barrier, depth - 1 + SIDE - 1 + ranks - 1)
+
+    for dy in range(1, SIDE):
+        pl.semaphore_signal(
+            column_in, inc=1, device_id={"vocab": z * SIDE + ys[dy]}, device_id_type=MESH
+        )
+    push_half(raw_ways, [0], False, True)
     for d in range(1, ranks):
         other = lax.rem(rank + d, ranks)
         pltpu.make_async_remote_copy(
@@ -129,20 +208,23 @@
             device_id={"state": other},
             device_id_type=MESH,
         ).start()
-
-    def push_raw(i, carry):
-        there, offset = peer(i, z, y, depth)
-        pltpu.make_async_remote_copy(
-            src_ref=send_raw.at[there],
-            dst_ref=got_raw.at[offset],
-            send_sem=raw_send,
-            recv_sem=raw_recv,
-            device_id={"vocab": there},
+    pl.semaphore_wait(column_in, SIDE - 1)
+
+    @pl.when(late != 0)
+    def _():
+        pl.semaphore_signal(
+            late_in,
+            inc=1,
+            device_id={"vocab": (depth - 1 - z) * SIDE + y},
             device_id_type=MESH,
-        ).start()
-        return carry
-
-    lax.fori_loop(0, owners - 1, push_raw, 0)
+        )
+
+    push_half(raw_ways, list(range(1, SIDE)), False, True)
+
+    @pl.when(late != 0)
+    def _():
+        push_half(raw_ways, list(range(SIDE)), True, False)
+
     own_raw = pltpu.make_async_copy(send_raw.at[me], got_raw.at[0], own_sem.at[0])
     own_raw.start()
 
@@ -170,27 +252,14 @@
     meta = jnp.where(lane == 3, jnp.sum(picks[0] * scale, axis=1, keepdims=True), meta)
     send_meta[...] = meta.reshape(owners, 1, LANES)
 
-    def push_pair(i, carry):
-        there, offset = peer(i, z, y, depth)
-        pltpu.make_async_remote_copy(
-            src_ref=send_pair.at[there],
-            dst_ref=got_pair.at[offset],
-            send_sem=pair_send,
-            recv_sem=pair_recv,
-            device_id={"vocab": there},
-            device_id_type=MESH,
-        ).start()
-        pltpu.make_async_remote_copy(
-            src_ref=send_meta.at[there],
-            dst_ref=got_meta.at[offset],
-            send_sem=meta_send,
-            recv_sem=meta_recv,
-            device_id={"vocab": there},
-            device_id_type=MESH,
-        ).start()
-        return carry
-
-    lax.fori_loop(0, owners - 1, push_pair, 0)
+    push_half(pair_ways, list(range(SIDE)), False, False)
+
+    @pl.when(late == 0)
+    def _():
+        pl.semaphore_wait(late_in, 1)
+        push_half(raw_ways, list(range(SIDE)), True, False)
+
+    push_half(pair_ways, list(range(SIDE)), True, False)
     own_pair = pltpu.make_async_copy(send_pair.at[me], got_pair.at[0], own_sem.at[1])
     own_pair.start()
     own_meta = pltpu.make_async_copy(send_meta.at[me], got_meta.at[0], own_sem.at[2])
@@ -251,9 +320,12 @@
             jax.ShapeDtypeStruct((owners, 2 * parts, LANES), BF16),
             jax.ShapeDtypeStruct((owners, 1, LANES), F32),
         ),
-        in_specs=[vmem] * 3,
+        in_specs=[pl.BlockSpec(memory_space=pltpu.HBM)] * 3,
         out_specs=(anywhere,) * 3,
         scratch_shapes=[
+            pltpu.VMEM((1, count), jnp.int32),
+            pltpu.VMEM((count, width), BF16),
+            pltpu.VMEM((count, width), BF16),
             pltpu.VMEM((count, width), BF16),
             pltpu.VMEM((owners * parts, LANES), F32),
             pltpu.VMEM((owners, parts, LANES), BF16),
@@ -269,11 +341,19 @@
             dma,
             dma,
             dma((3,)),
+            dma((3,)),
+            pltpu.SemaphoreType.REGULAR,
+            pltpu.SemaphoreType.REGULAR,
         ],
         compiler_params=pltpu.CompilerParams(
             collective_id=0, has_side_effects=True, vmem_limit_bytes=32 * 1024 * 1024
         ),
-    )(token_ids.reshape(1, count), forward_rows, backward_rows)
+    )(
+        *(
+            pltpu.with_memory_space_constraint(operand, pltpu.HBM)
+            for operand in (token_ids.reshape(1, count), forward_rows, backward_rows)
+        )
+    )
     return pl.pallas_call(
         place,
         out_shape=jax.ShapeDtypeStruct((width, V_DEV), BF16),

time: 61.1 us -> 57.3 us (0.938); the launches traced: 60 us -> 57.1 us
  local copies, waits for them, and re-layouts: 2.71 us -> 0 us
    unnamed x6 -> x0, local copies, waits for them, and re-layouts: 2.71 us -> none
where the time goes in v2:
time: 57.3 us; the launch traced here: 57.1 us
  Pallas kernels  57.1 us (100%)
    pallas_call x1, Pallas kernels, shards(): pl.pallas_call(functools.partial(exchange, owners, ranks), out_shape=(jax...  53.7 us
    pallas_call x1, Pallas kernels, shards(): pl.pallas_call(place, out_shape=jax.ShapeDtypeStruct((width, V_DEV), BF16...  3.4 us

profile of v2, /device:TPU:24, one launch (start us, length us, event | category | flops | bytes accessed | tf_op | source)
XLA Modules:
  0.0 57.1 jit_solution(5720444179376857358)
XLA Ops:
  0.0 53.7 %shard_map.37 = (bf16[64,16,128]{2,1,0:T(8,128)(2,1)S(1)}, bf16[64,32,128]{2,1,0:T(8,128)(2,1)S(1)}, f32[64,1,128]{2,1,0:T(1,128)S(1)}) custom-call(s32[1,120]{1,0:T(1,128)} %bitcast.1, bf16[120,2048]{1,0:T(8,128)(2,1)} %forward_ref.1, bf16[120,2048]{1,0:T(8,128)(2,1)} %backward_ref.1), custom_call_target="tpu_custom_call" | custom-call | tf_op jit(solution)/shard_map/pallas_call | solution.py:316
  53.7 3.4 %shard_map.38 = bf16[2048,1024]{1,0:T(8,128)(2,1)} custom-call(bf16[64,16,128]{2,1,0:T(8,128)(2,1)S(1)} %get-tuple-element.8.raw_ref, bf16[64,32,128]{2,1,0:T(8,128)(2,1)S(1)} %get-tuple-element.9.pair_ref, f32[64,1,128]{2,1,0:T(1,128)S(1)} %get-tuple-element.10.meta_ref), custom_call_target="tpu_custom_call" | custom-call | tf_op jit(solution)/shard_map/pallas_call | solution.py:357

commit v3 on v2

--- a/solution.py
+++ b/solution.py
@@ -15,14 +15,19 @@
 BF16 = jnp.bfloat16
 
 
-def target(k, z, half, to_late):
+def hop(k, z, depth):
+    half = depth // 2
     late = z // half
-    h = (k + 1) // 2
-    turn = h * (1 - 2 * lax.rem(k, 2)) + 2 * half
-    if to_late:
-        return half + lax.rem(z + turn + late * (half // 2), half)
-    ranked = lax.rem(k, 2) * (half // 2) + k // 2
-    return (1 - late) * lax.rem(z + turn + half // 2, half) + late * ranked
+    last = k // (depth - 1)
+    j = k // 2
+    minus = lax.rem(k, 2)
+    up = half - j
+    down = half - 1 - j
+    return lax.rem((1 - minus) * up + minus * (depth - down), depth)
+
+
+def column_order(k, z, depth):
+    return k // 2 + lax.rem(k, 2) * (depth // 2)
 
 
 def route(token_row):
@@ -91,7 +96,6 @@
     own_sem,
     load_sem,
     column_in,
-    late_in,
 ):
     depth = owners // SIDE
     me = lax.axis_index("vocab")
@@ -108,8 +112,6 @@
     for load in loads:
         load.start()
 
-    half = depth // 2
-    late = z // half
     ys = [lax.rem(y + dy, SIDE) for dy in range(SIDE)]
 
     barrier = pltpu.get_barrier_semaphore()
@@ -117,14 +119,8 @@
     def greet(**where):
         pl.semaphore_signal(barrier, inc=1, device_id=where, device_id_type=MESH)
 
-    for dz in range(1, half):
-        greet(vocab=(late * half + lax.rem(z + dz, half)) * SIDE + y)
-
-    @pl.when(late == 0)
-    def _():
-        for k in range(half):
-            greet(vocab=(half + k) * SIDE + y)
-
+    for dz in range(1, depth):
+        greet(vocab=lax.rem(z + dz, depth) * SIDE + y)
     for dy in range(1, SIDE):
         greet(vocab=z * SIDE + ys[dy])
     for d in range(1, ranks):
@@ -147,37 +143,46 @@
     )
     sums[rank] = partial[:1]
 
-    def push(sources, k, dys, to_late):
-        there_z = target(k, z, half, to_late)
-        dz = lax.rem(there_z - z + depth, depth)
+    def send(sources, there_z, dz, dy):
+        there = there_z * SIDE + ys[dy]
+        for source, landing, sent, landed in sources:
+            pltpu.make_async_remote_copy(
+                src_ref=source.at[there],
+                dst_ref=landing.at[dz * SIDE + dy],
+                send_sem=sent,
+                recv_sem=landed,
+                device_id={"vocab": there},
+                device_id_type=MESH,
+            ).start()
+
+    def push(sources, k, dys):
+        dz = hop(k, z, depth)
+        there_z = lax.rem(z + dz, depth)
         for dy in dys:
-            there = there_z * SIDE + ys[dy]
-            for source, landing, sent, landed in sources:
-                pltpu.make_async_remote_copy(
-                    src_ref=source.at[there],
-                    dst_ref=landing.at[dz * SIDE + dy],
-                    send_sem=sent,
-                    recv_sem=landed,
-                    device_id={"vocab": there},
-                    device_id_type=MESH,
-                ).start()
-
-    def push_half(sources, dys, to_late, unroll):
+            send(sources, there_z, dz, dy)
+
+    def push_all(sources, dys):
         def step(k, carry):
-            push(sources, k, dys, to_late)
+            push(sources, k, dys)
             return carry
 
-        if unroll:
-            for k in range(half - 1):
-                push(sources, k, dys, to_late)
-        else:
-            lax.fori_loop(0, half - 1, step, 0)
-        push(sources, half - 1, [dy for dy in dys if dy], to_late)
-        if 0 in dys:
-
-            @pl.when(late != int(to_late))
+        lax.fori_loop(0, depth - 1, step, 0)
+        push(sources, depth - 1, [dy for dy in dys if dy])
+
+    def push_column(sources):
+        def step(k, carry):
+            there_z = column_order(k, z, depth)
+            dz = lax.rem(there_z - z + depth, depth)
+
+            @pl.when(dz != 0)
             def _():
-                push(sources, half - 1, [0], to_late)
+                send(sources, there_z, dz, 0)
+
+            for dy in range(1, SIDE):
+                send(sources, there_z, dz, dy)
+            return carry
+
+        lax.fori_loop(0, depth, step, 0)
 
     raw_ways = ((send_raw, got_raw, raw_send, raw_recv),)
     pair_ways = (
@@ -185,19 +190,13 @@
         (send_meta, got_meta, meta_send, meta_recv),
     )
 
-    @pl.when(late == 0)
-    def _():
-        pl.semaphore_wait(barrier, half - 1 + SIDE - 1 + ranks - 1)
-
-    @pl.when(late != 0)
-    def _():
-        pl.semaphore_wait(barrier, depth - 1 + SIDE - 1 + ranks - 1)
+    pl.semaphore_wait(barrier, depth - 1 + SIDE - 1 + ranks - 1)
 
     for dy in range(1, SIDE):
         pl.semaphore_signal(
             column_in, inc=1, device_id={"vocab": z * SIDE + ys[dy]}, device_id_type=MESH
         )
-    push_half(raw_ways, [0], False, True)
+    push_all(raw_ways, [0])
     for d in range(1, ranks):
         other = lax.rem(rank + d, ranks)
         pltpu.make_async_remote_copy(
@@ -210,21 +209,7 @@
         ).start()
     pl.semaphore_wait(column_in, SIDE - 1)
 
-    @pl.when(late != 0)
-    def _():
-        pl.semaphore_signal(
-            late_in,
-            inc=1,
-            device_id={"vocab": (depth - 1 - z) * SIDE + y},
-            device_id_type=MESH,
-        )
-
-    push_half(raw_ways, list(range(1, SIDE)), False, True)
-
-    @pl.when(late != 0)
-    def _():
-        push_half(raw_ways, list(range(SIDE)), True, False)
-
+    push_all(raw_ways, list(range(1, SIDE)))
     own_raw = pltpu.make_async_copy(send_raw.at[me], got_raw.at[0], own_sem.at[0])
     own_raw.start()
 
@@ -252,14 +237,7 @@
     meta = jnp.where(lane == 3, jnp.sum(picks[0] * scale, axis=1, keepdims=True), meta)
     send_meta[...] = meta.reshape(owners, 1, LANES)
 
-    push_half(pair_ways, list(range(SIDE)), False, False)
-
-    @pl.when(late == 0)
-    def _():
-        pl.semaphore_wait(late_in, 1)
-        push_half(raw_ways, list(range(SIDE)), True, False)
-
-    push_half(pair_ways, list(range(SIDE)), True, False)
+    push_column(pair_ways)
     own_pair = pltpu.make_async_copy(send_pair.at[me], got_pair.at[0], own_sem.at[1])
     own_pair.start()
     own_meta = pltpu.make_async_copy(send_meta.at[me], got_meta.at[0], own_sem.at[2])
@@ -279,8 +257,10 @@
 
 def place(raw_ref, pair_ref, meta_ref, out_ref, wide_raw, wide_pair, onehot, block, sems):
     owners, parts, _ = raw_ref.shape
-    wide_raw[...] = raw_ref[...].reshape(owners * parts, LANES).astype(F32)
-    wide_pair[...] = pair_ref[...].reshape(owners * 2 * parts, LANES).astype(F32)
+    odd, odd_pair = parts + 1, 2 * parts + 1
+    for k in range(owners):
+        wide_raw[k * odd : k * odd + parts, :] = raw_ref[k].astype(F32)
+        wide_pair[k * odd_pair : k * odd_pair + 2 * parts, :] = pair_ref[k].astype(F32)
     meta = meta_ref[...].reshape(owners, LANES)
     ids = lax.broadcasted_iota(jnp.int32, (owners, V_DEV), 1).astype(F32)
     for s in range(3):
@@ -289,9 +269,9 @@
     scale = meta[:, 3:4]
     copies = []
     for i in range(parts):
-        lone = wide_raw[pl.ds(i, owners, stride=parts), :] * scale
-        one = wide_pair[pl.ds(i, owners, stride=2 * parts), :]
-        two = wide_pair[pl.ds(parts + i, owners, stride=2 * parts), :]
+        lone = wide_raw[pl.ds(i, owners, stride=odd), :] * scale
+        one = wide_pair[pl.ds(i, owners, stride=odd_pair), :]
+        two = wide_pair[pl.ds(parts + i, owners, stride=odd_pair), :]
         rows = jnp.concatenate([lone.astype(BF16), one.astype(BF16), two.astype(BF16)], axis=0)
         counts = lax.dot_general(
             rows, onehot[...], (((0,), (0,)), ((), ())), preferred_element_type=F32
@@ -343,7 +323,6 @@
             dma((3,)),
             dma((3,)),
             pltpu.SemaphoreType.REGULAR,
-            pltpu.SemaphoreType.REGULAR,
         ],
         compiler_params=pltpu.CompilerParams(
             collective_id=0, has_side_effects=True, vmem_limit_bytes=32 * 1024 * 1024
@@ -360,8 +339,8 @@
         in_specs=[vmem] * 3,
         out_specs=anywhere,
         scratch_shapes=[
-            pltpu.VMEM((owners * parts, LANES), F32),
-            pltpu.VMEM((owners * 2 * parts, LANES), F32),
+            pltpu.VMEM((owners * (parts + 1), LANES), F32),
+            pltpu.VMEM((owners * (2 * parts + 1), LANES), F32),
             pltpu.VMEM((3 * owners, V_DEV), BF16),
             pltpu.VMEM((width, V_DEV), BF16),
             dma((parts,)),

time: 57.3 us -> 53.7 us (0.937)
  the two profiles are of different devices: /device:TPU:24 before, /device:TPU:192 now
where the time goes in v3:
time: 53.7 us; the launch traced here: 53.6 us
  Pallas kernels  53.6 us (100%)
    pallas_call x1, Pallas kernels, shards(): pl.pallas_call(functools.partial(exchange, owners, ranks), out_shape=(jax...  50.7 us
    pallas_call x1, Pallas kernels, shards(): pl.pallas_call(place, out_shape=jax.ShapeDtypeStruct((width, V_DEV), BF16...  2.85 us

profile of v3, /device:TPU:192, one launch (start us, length us, event | category | flops | bytes accessed | tf_op | source)
XLA Modules:
  0.0 53.6 jit_solution(14399284059838098326)
XLA Ops:
  0.0 50.7 %shard_map.37 = (bf16[64,16,128]{2,1,0:T(8,128)(2,1)S(1)}, bf16[64,32,128]{2,1,0:T(8,128)(2,1)S(1)}, f32[64,1,128]{2,1,0:T(1,128)S(1)}) custom-call(s32[1,120]{1,0:T(1,128)} %bitcast.1, bf16[120,2048]{1,0:T(8,128)(2,1)} %forward_ref.1, bf16[120,2048]{1,0:T(8,128)(2,1)} %backward_ref.1), custom_call_target="tpu_custom_call" | custom-call | tf_op jit(solution)/shard_map/pallas_call | solution.py:296
  50.7 2.8 %shard_map.38 = bf16[2048,1024]{1,0:T(8,128)(2,1)} custom-call(bf16[64,16,128]{2,1,0:T(8,128)(2,1)S(1)} %get-tuple-element.8.raw_ref, bf16[64,32,128]{2,1,0:T(8,128)(2,1)S(1)} %get-tuple-element.9.pair_ref, f32[64,1,128]{2,1,0:T(1,128)S(1)} %get-tuple-element.10.meta_ref), custom_call_target="tpu_custom_call" | custom-call | tf_op jit(solution)/shard_map/pallas_call | solution.py:336

commit v4 on v3

--- a/solution.py
+++ b/solution.py
@@ -26,7 +26,7 @@
     return lax.rem((1 - minus) * up + minus * (depth - down), depth)
 
 
-def column_order(k, z, depth):
+def column_order(k, depth):
     return k // 2 + lax.rem(k, 2) * (depth // 2)
 
 
@@ -138,13 +138,8 @@
     raw = jnp.dot(picks[0].astype(BF16), weights[...], preferred_element_type=F32)
     lay(raw, wide, send_raw, 0)
 
-    partial = lax.dot_general(
-        jnp.ones((8, width), BF16), weights[...], (((1,), (1,)), ((), ())), preferred_element_type=F32
-    )
-    sums[rank] = partial[:1]
-
-    def send(sources, there_z, dz, dy):
-        there = there_z * SIDE + ys[dy]
+    def send(sources, there_z, dz, dy, there_y):
+        there = there_z * SIDE + there_y
         for source, landing, sent, landed in sources:
             pltpu.make_async_remote_copy(
                 src_ref=source.at[there],
@@ -159,7 +154,7 @@
         dz = hop(k, z, depth)
         there_z = lax.rem(z + dz, depth)
         for dy in dys:
-            send(sources, there_z, dz, dy)
+            send(sources, there_z, dz, dy, ys[dy])
 
     def push_all(sources, dys):
         def step(k, carry):
@@ -170,19 +165,34 @@
         push(sources, depth - 1, [dy for dy in dys if dy])
 
     def push_column(sources):
+        lead = depth // 4
+
+        def reach(k, theres):
+            there_z = column_order(k, depth)
+            dz = lax.rem(there_z - z + depth, depth)
+            for there_y in theres:
+                dy = lax.rem(there_y - y + SIDE, SIDE)
+
+                @pl.when(dz + dy != 0)
+                def _(there_y=there_y, dy=dy):
+                    send(sources, there_z, dz, dy, there_y)
+
+        def begin(k, carry):
+            reach(k, (0,))
+            return carry
+
         def step(k, carry):
-            there_z = column_order(k, z, depth)
-            dz = lax.rem(there_z - z + depth, depth)
-
-            @pl.when(dz != 0)
-            def _():
-                send(sources, there_z, dz, 0)
-
-            for dy in range(1, SIDE):
-                send(sources, there_z, dz, dy)
+            reach(k + lead, (0,))
+            reach(k, range(1, SIDE))
             return carry
 
-        lax.fori_loop(0, depth, step, 0)
+        def finish(k, carry):
+            reach(k, range(1, SIDE))
+            return carry
+
+        lax.fori_loop(0, lead, begin, 0)
+        lax.fori_loop(0, depth - lead, step, 0)
+        lax.fori_loop(depth - lead, depth, finish, 0)
 
     raw_ways = ((send_raw, got_raw, raw_send, raw_recv),)
     pair_ways = (
@@ -197,6 +207,10 @@
             column_in, inc=1, device_id={"vocab": z * SIDE + ys[dy]}, device_id_type=MESH
         )
     push_all(raw_ways, [0])
+    partial = lax.dot_general(
+        jnp.ones((8, width), BF16), weights[...], (((1,), (1,)), ((), ())), preferred_element_type=F32
+    )
+    sums[rank] = partial[:1]
     for d in range(1, ranks):
         other = lax.rem(rank + d, ranks)
         pltpu.make_async_remote_copy(

time: 53.7 us -> 52.7 us (0.981)
  the two profiles are of different devices: /device:TPU:192 before, /device:TPU:200 now
where the time goes in v4:
time: 52.7 us; the launch traced here: 52.6 us
  Pallas kernels  52.6 us (100%)
    pallas_call x1, Pallas kernels, shards(): pl.pallas_call(functools.partial(exchange, owners, ranks), out_shape=(jax...  49.7 us
    pallas_call x1, Pallas kernels, shards(): pl.pallas_call(place, out_shape=jax.ShapeDtypeStruct((width, V_DEV), BF16...  2.84 us

profile of v4, /device:TPU:200, one launch (start us, length us, event | category | flops | bytes accessed | tf_op | source)
XLA Modules:
  0.0 52.6 jit_solution(4892592600091486059)
XLA Ops:
  0.0 49.7 %shard_map.37 = (bf16[64,16,128]{2,1,0:T(8,128)(2,1)S(1)}, bf16[64,32,128]{2,1,0:T(8,128)(2,1)S(1)}, f32[64,1,128]{2,1,0:T(1,128)S(1)}) custom-call(s32[1,120]{1,0:T(1,128)} %bitcast.1, bf16[120,2048]{1,0:T(8,128)(2,1)} %forward_ref.1, bf16[120,2048]{1,0:T(8,128)(2,1)} %backward_ref.1), custom_call_target="tpu_custom_call" | custom-call | tf_op jit(solution)/shard_map/pallas_call | solution.py:310
  49.7 2.8 %shard_map.38 = bf16[2048,1024]{1,0:T(8,128)(2,1)} custom-call(bf16[64,16,128]{2,1,0:T(8,128)(2,1)S(1)} %get-tuple-element.8.raw_ref, bf16[64,32,128]{2,1,0:T(8,128)(2,1)S(1)} %get-tuple-element.9.pair_ref, f32[64,1,128]{2,1,0:T(1,128)S(1)} %get-tuple-element.10.meta_ref), custom_call_target="tpu_custom_call" | custom-call | tf_op jit(solution)/shard_map/pallas_call | solution.py:350

commit v5 on v4

--- a/solution.py
+++ b/solution.py
@@ -64,7 +64,7 @@
     parts = width // LANES
     for i in range(parts):
         wide[pl.ds(i, k, stride=parts), :] = rows[:, i * LANES : (i + 1) * LANES]
-    out[:, base : base + parts, :] = wide[...].reshape(k, parts, LANES).astype(BF16)
+    out[:, base : base + parts, :] = wide[: k * parts, :].reshape(k, parts, LANES).astype(BF16)
 
 
 def exchange(
@@ -321,7 +321,7 @@
             pltpu.VMEM((count, width), BF16),
             pltpu.VMEM((count, width), BF16),
             pltpu.VMEM((count, width), BF16),
-            pltpu.VMEM((owners * parts, LANES), F32),
+            pltpu.VMEM(((owners + 1) * parts, LANES), F32),
             pltpu.VMEM((owners, parts, LANES), BF16),
             pltpu.VMEM((owners, 2 * parts, LANES), BF16),
             pltpu.VMEM((owners, 1, LANES), F32),
@@ -353,8 +353,8 @@
         in_specs=[vmem] * 3,
         out_specs=anywhere,
         scratch_shapes=[
-            pltpu.VMEM((owners * (parts + 1), LANES), F32),
-            pltpu.VMEM((owners * (2 * parts + 1), LANES), F32),
+            pltpu.VMEM(((owners + 1) * (parts + 1), LANES), F32),
+            pltpu.VMEM(((owners + 1) * (2 * parts + 1), LANES), F32),
             pltpu.VMEM((3 * owners, V_DEV), BF16),
             pltpu.VMEM((width, V_DEV), BF16),
             dma((parts,)),

time: 52.7 us -> 52.7 us (level)
  no operation moved by 1% of the time
where the time goes in v5:
time: 52.7 us; the launch traced here: 52.6 us
  Pallas kernels  52.6 us (100%)
    pallas_call x1, Pallas kernels, shards(): pl.pallas_call(functools.partial(exchange, owners, ranks), out_shape=(jax...  49.7 us
    pallas_call x1, Pallas kernels, shards(): pl.pallas_call(place, out_shape=jax.ShapeDtypeStruct((width, V_DEV), BF16...  2.84 us

profile of v5, /device:TPU:200, one launch (start us, length us, event | category | flops | bytes accessed | tf_op | source)
XLA Modules:
  0.0 52.6 jit_solution(1113415321435738374)
XLA Ops:
  0.0 49.7 %shard_map.37 = (bf16[64,16,128]{2,1,0:T(8,128)(2,1)S(1)}, bf16[64,32,128]{2,1,0:T(8,128)(2,1)S(1)}, f32[64,1,128]{2,1,0:T(1,128)S(1)}) custom-call(s32[1,120]{1,0:T(1,128)} %bitcast.1, bf16[120,2048]{1,0:T(8,128)(2,1)} %forward_ref.1, bf16[120,2048]{1,0:T(8,128)(2,1)} %backward_ref.1), custom_call_target="tpu_custom_call" | custom-call | tf_op jit(solution)/shard_map/pallas_call | solution.py:310
  49.7 2.8 %shard_map.38 = bf16[2048,1024]{1,0:T(8,128)(2,1)} custom-call(bf16[64,16,128]{2,1,0:T(8,128)(2,1)S(1)} %get-tuple-element.8.raw_ref, bf16[64,32,128]{2,1,0:T(8,128)(2,1)S(1)} %get-tuple-element.9.pair_ref, f32[64,1,128]{2,1,0:T(1,128)S(1)} %get-tuple-element.10.meta_ref), custom_call_target="tpu_custom_call" | custom-call | tf_op jit(solution)/shard_map/pallas_call | solution.py:350
